TPU v7x, 256 devices: a whole 4x4x8 slice. The times are simulated.
256 devices in a mesh: gx: 8 (over z), gy: 32 (over y, x, core).
Axes of the slice: x: 4, y: 4, z: 8, core: 2. Of those that a mesh axis runs over, the one named last changes fastest.
Arguments:
- start_charges: float32 [65536, 128], P(('gx', 'gy'))
- solute_field: float32 [65536, 128], P(('gx', 'gy'))
- exposure: float32 [65536, 128], P(('gx', 'gy')), may hold values from 0 to 1
- owner_offset: int32 [65536, 32], P(('gx', 'gy')), may hold values from 0 to 8, as said below
- owner_row: int32 [65536, 32], P(('gx', 'gy')), may hold values from 0 to 255, as said below
- live_slots: int32 [65536, 4], P(('gx', 'gy')), may hold values from 0 to 8
- coupling: float32 [65536, 32], P(('gx', 'gy')), may hold values from 0.02 to 0.2
- cell_index: int32 [65536], P(('gx', 'gy')), may hold values from 0 to 1023, never falling along the last dimension, each value on 1 to 128 neighbouring positions
- evaluation: float32 [512, 128], replicated
- projection: float32 [128, 128], replicated
- far_kernel: float32 [1024, 1024], replicated, may hold values from -0.01171875 to 0.01171875
Outputs:
- final_charges: float32 [65536, 128], P(('gx', 'gy'))
Inputs may be any that keep to these rules, and one draw needn't show every extreme that they name: `owner_offset`: A neighbour lies on the sphere's own device (offset 4) or on a device beside it or across a corner in the 8 x 32 grid of devices; no offset leaves the grid. `owner_row`: A neighbour on another device is among the first 64 spheres of that device. `cell_index`: cell numbers never fall along the spheres; each cell holds 1 to 128 spheres.
All inputs are finite; a program needn't handle non-finite values.
Results may differ from a plain program's by a relative error of at most 0.0003.
Values sent between devices are 32-bit elements; how exact they have to be, the bound alone decides.
A program may use at most 64 MiB of HBM per device.

v0:
```python
import math

import jax
import jax.numpy as jnp
from jax import lax
from jax.sharding import PartitionSpec as P

LMAX = 10
H = 128
Q = 16
ND = 4
SLOTS = 8
NB = 32
EDGE = 64
ITERS = 4


def padded(value, sides, width):
    for axis, dim in sides:
        devices, length = (lax.axis_size(axis), value.shape[dim])
        up = [(i, (i + 1) % devices) for i in range(devices - 1)]
        down = [(j, i) for i, j in up]
        last = lax.slice_in_dim(value, length - width, length, axis=dim)
        initial = lax.slice_in_dim(value, 0, width, axis=dim)
        before = lax.ppermute(last, axis, up)
        after = lax.ppermute(initial, axis, down)
        value = jnp.concatenate([before, value, after], axis=dim)
    return value


def degree_scale():
    index = jnp.arange(H, dtype=jnp.int32)
    bounds = jnp.arange(1, LMAX + 1, dtype=jnp.int32) ** 2
    degree = jnp.sum((index[:, None] >= bounds[None, :]).astype(jnp.int32), axis=1)
    values = (2.0 * degree.astype(jnp.float32) + 1.0) / (4.0 * math.pi)
    return jnp.where(index < (LMAX + 1) ** 2, values, jnp.float32(0.0))


def spd_mixing(margins):
    order = len(margins)
    diagonal_sum = margins[0][0]
    for a in range(1, order):
        diagonal_sum = diagonal_sum + margins[a][a]
    damping = 0.01 * diagonal_sum / order
    triangle = [[None] * order for a in range(order)]
    for a in range(order):
        for b in range(a + 1):
            running = margins[a][b] + (damping if a == b else 0.0)
            for c in range(b):
                running = running - triangle[a][c] * triangle[b][c]
            if a == b:
                triangle[a][a] = jnp.sqrt(running)
            else:
                triangle[a][b] = running / triangle[b][b]
    forward = []
    for a in range(order):
        running = jnp.float32(1.0)
        for c in range(a):
            running = running - triangle[a][c] * forward[c]
        forward.append(running / triangle[a][a])
    backward = [None] * order
    for a in reversed(range(order)):
        running = forward[a]
        for c in range(a + 1, order):
            running = running - triangle[c][a] * backward[c]
        backward[a] = running / triangle[a][a]
    weight_sum = backward[0]
    for a in range(1, order):
        weight_sum = weight_sum + backward[a]
    return [value / weight_sum for value in backward]


def combine_list(mixing, items):
    mixed = mixing[0] * items[0]
    for a in range(1, len(items)):
        mixed = mixed + mixing[a] * items[a]
    return mixed


def drop_centre(beside_all):
    blocks_nine = beside_all.reshape(9, EDGE, H)
    return jnp.concatenate([blocks_nine[:4], blocks_nine[5:]], axis=0).reshape(8 * EDGE, H)


def remote_rows(charges):
    export = charges[:EDGE].reshape(1, 1, EDGE, H)
    beside_all = padded(export, (("gx", 0), ("gy", 1)), 1)
    return drop_centre(beside_all)


def per_device(
    start_charges,
    solute_field,
    exposure,
    owner_offset,
    owner_row,
    live_slots,
    coupling,
    cell_index,
    evaluation,
    projection,
    far_kernel,
):
    highest = lax.Precision.HIGHEST
    spheres = start_charges.shape[0]
    cells = far_kernel.shape[0]
    scale = degree_scale()
    offset_code = jnp.where(owner_offset > 4, owner_offset - 1, owner_offset)
    positions = jnp.where(owner_offset == 4, owner_row, spheres + offset_code * EDGE + owner_row)
    slot_index = jnp.arange(NB, dtype=jnp.int32) % SLOTS
    live = slot_index[None, :] < jnp.repeat(live_slots, SLOTS, axis=1)
    weights = jnp.where(live, coupling, jnp.float32(0.0))
    membership = (cell_index[:, None] == jnp.arange(cells, dtype=jnp.int32)[None, :]).astype(
        jnp.float32
    )

    def class_sum(sources, d):
        gathered = sources[positions[:, d * SLOTS : (d + 1) * SLOTS]]
        return jnp.einsum(
            "ks,ksh->kh", weights[:, d * SLOTS : (d + 1) * SLOTS], gathered, precision=highest
        )

    def jacobi_map(sources, moments):
        classes = jnp.concatenate([class_sum(sources, d) for d in range(ND)], axis=1)
        potential = jnp.dot(classes, evaluation, precision=highest)
        nearby = jnp.dot(potential * exposure, projection, precision=highest)
        expansion = jnp.dot(moments, far_kernel, precision=highest)
        distant = jnp.dot(membership, expansion.T, precision=highest)
        distant = jnp.pad(distant, ((0, 0), (0, H - Q)))
        return scale[None, :] * (solute_field - nearby - distant)

    charges = start_charges
    history = []
    changes = []
    rows_list = []
    for t in range(ITERS):
        moments = lax.psum(jnp.dot(charges[:, :Q].T, membership, precision=highest), ("gx", "gy"))
        sources = jnp.concatenate([charges, remote_rows(charges)], axis=0)
        updated = jacobi_map(sources, moments)
        change = updated - charges
        history.append(updated)
        changes.append(change)
        products = jnp.stack([jnp.sum(change * other_change) for other_change in changes])
        margin_values = lax.psum(products, ("gx", "gy"))
        rows_list.append([margin_values[a] for a in range(t + 1)])
        margins = [[rows_list[max(a, b)][min(a, b)] for b in range(t + 1)] for a in range(t + 1)]
        mixing = spd_mixing(margins)
        charges = combine_list(mixing, history)
    return charges


def solution(mesh):
    placed = (
        P(("gx", "gy"), None),
        P(("gx", "gy"), None),
        P(("gx", "gy"), None),
        P(("gx", "gy"), None),
        P(("gx", "gy"), None),
        P(("gx", "gy"), None),
        P(("gx", "gy"), None),
        P(("gx", "gy")),
        P(),
        P(),
        P(),
    )
    return jax.shard_map(
        per_device, mesh=mesh, in_specs=placed, out_specs=P(("gx", "gy"), None), check_vma=False
    )
```

profile of v0, /device:TPU:1, one launch (start us, length us, event | category | flops | bytes accessed | tf_op | source)
XLA Modules:
  0.0 1504.9 jit_solution(10966037728120528556)
XLA Ops:
  18.5 239.9 %all-reduce.9.cloned.1.call-done = f32[16,1024]{1,0:T(8,128)} async-done(((f32[16,1024]{1,0:T(8,128)}), f32[16,1024]{1,0:T(8,128)}) %all-reduce.9.cloned.1.call-update) | async-done | bytes 65552 | tf_op jit(solution)/shard_map/psum | solution.py:137
  271.3 7.6 gather_fusion.1
  278.9 7.6 gather_fusion.2
  286.4 5.5 gather_fusion
  291.9 5.5 gather_fusion.3
  309.3 76.3 %psum.57 = f32[]{:T(128)} all-reduce(f32[]{:T(128)} %get-tuple-element.16), channel_id=1, replica_groups=mesh['gx'=8,'gy'=32] {'gx','gy'}, use_global_device_ids=true, to_apply=%region_3.4 | all-reduce | flops 1 | bytes 8 | tf_op jit(solution)/shard_map/psum | solution.py:144
  393.4 228.7 %all-reduce.11.cloned.1.call-done = f32[16,1024]{1,0:T(8,128)} async-done(((f32[16,1024]{1,0:T(8,128)}), f32[16,1024]{1,0:T(8,128)}) %all-reduce.11.cloned.1.call-update) | async-done | bytes 65552 | tf_op jit(solution)/shard_map/psum | solution.py:137
  635.1 7.6 gather_fusion.4
  642.6 7.6 gather_fusion.5
  650.2 5.5 gather_fusion.6
  655.7 5.5 gather_fusion.7
  674.6 76.5 %psum.59 = f32[2]{0:T(128)S(1)} all-reduce(f32[2]{0:T(128)S(1)} %pad_maximum_fusion.16), channel_id=1, replica_groups=mesh['gx'=8,'gy'=32] {'gx','gy'}, use_global_device_ids=true, to_apply=%region_7.8 | all-reduce | flops 2 | bytes 16 | tf_op jit(solution)/shard_map/psum | solution.py:144
  761.3 229.0 %all-reduce.13.cloned.1.call-done = f32[16,1024]{1,0:T(8,128)} async-done(((f32[16,1024]{1,0:T(8,128)}), f32[16,1024]{1,0:T(8,128)}) %all-reduce.13.cloned.1.call-update) | async-done | bytes 65552 | tf_op jit(solution)/shard_map/psum | solution.py:137
  1003.3 7.6 gather_fusion.8
  1010.8 7.6 gather_fusion.9
  1018.4 5.5 gather_fusion.10
  1023.9 5.5 gather_fusion.11
  1043.1 76.3 %psum.61 = f32[3]{0:T(128)S(1)} all-reduce(f32[3]{0:T(128)S(1)} %pad_maximum_fusion.17), channel_id=1, replica_groups=mesh['gx'=8,'gy'=32] {'gx','gy'}, use_global_device_ids=true, to_apply=%region_12.13 | all-reduce | flops 3 | bytes 24 | tf_op jit(solution)/shard_map/psum | solution.py:144
  1131.2 228.8 %all-reduce.15.cloned.1.call-done = f32[16,1024]{1,0:T(8,128)} async-done(((f32[16,1024]{1,0:T(8,128)}), f32[16,1024]{1,0:T(8,128)}) %all-reduce.15.cloned.1.call-update) | async-done | bytes 65552 | tf_op jit(solution)/shard_map/psum | solution.py:137
  1373.0 7.6 gather_fusion.12
  1380.6 7.6 gather_fusion.13
  1388.2 5.5 gather_fusion.14
  1393.6 5.5 gather_fusion.15
  1413.1 76.3 %psum.63 = f32[4]{0:T(128)S(1)} all-reduce(f32[4]{0:T(128)S(1)} %pad_maximum_fusion.18), channel_id=1, replica_groups=mesh['gx'=8,'gy'=32] {'gx','gy'}, use_global_device_ids=true, to_apply=%region_18.19 | all-reduce | flops 4 | bytes 32 | tf_op jit(solution)/shard_map/psum | solution.py:144
  (203 shorter events, 137.6 us)
Async XLA Ops:
  6.5 300.6 %copy-start = (f32[512,128]{1,0:T(8,128)S(1)}, f32[512,128]{1,0:T(8,128)}, u32[]{:S(2)}) copy-start(f32[512,128]{1,0:T(8,128)} %param.19) | copy-start | bytes 786436
  6.5 260.8 %copy-start.33 = (s32[256]{0:T(256)S(1)}, s32[256]{0:T(256)}, u32[]{:S(2)}) copy-start(s32[256]{0:T(256)} %param.18) | copy-start | bytes 3076
  6.5 251.8 %all-reduce.9.cloned.1.call-start = ((), (), s32[]{:S(2)}) async-start(), calls=%async_computation | async-start | bytes 131072 | tf_op jit(solution)/shard_map/psum | solution.py:137
  7.4 255.3 %collective-permute-start = (f32[1,1,64,128]{3,2,1,0:T(8,128)S(1)}, f32[1,1,64,128]{3,2,1,0:T(8,128)S(1)}, u32[]{:S(2)}, u32[]{:S(2)}) collective-permute-start(f32[1,1,64,128]{3,2,1,0:T(8,128)S(1)} %slice_bitcast_fusion.3), channel_id=1, source_target_pairs={{0,32},{32,64},{64,96},{96,128},{128,160},{160,192},{192,224},{1,3... | collective-permute-start | bytes 98312 | tf_op jit(solution)/shard_map/ppermute | solution.py:25
  11.7 250.9 %collective-permute-start.1 = (f32[1,1,64,128]{3,2,1,0:T(8,128)S(1)}, f32[1,1,64,128]{3,2,1,0:T(8,128)S(1)}, u32[]{:S(2)}, u32[]{:S(2)}) collective-permute-start(f32[1,1,64,128]{3,2,1,0:T(8,128)S(1)} %slice_bitcast_fusion.3), channel_id=1, source_target_pairs={{32,0},{64,32},{96,64},{128,96},{160,128},{192,160},{224,192},{33,... | collective-permute-start | bytes 98312 | tf_op jit(solution)/shard_map/ppermute | solution.py:26
  15.1 607.0 %all-reduce.11.cloned.1.call-start = ((), (), s32[]{:S(2)}) async-start(), calls=%async_computation.1 | async-start | bytes 131072 | tf_op jit(solution)/shard_map/psum | solution.py:137
  262.7 6.0 collective-permute-start.2
  265.2 5.9 collective-permute-start.3
  388.0 602.3 %all-reduce.13.cloned.1.call-start = ((), (), s32[]{:S(2)}) async-start(), calls=%async_computation.2 | async-start | bytes 131072 | tf_op jit(solution)/shard_map/psum | solution.py:137
  388.0 238.4 %collective-permute-start.4 = (f32[1,1,64,128]{3,2,1,0:T(8,128)S(1)}, f32[1,1,64,128]{3,2,1,0:T(8,128)S(1)}, u32[]{:S(2)}, u32[]{:S(2)}) collective-permute-start(f32[1,1,64,128]{3,2,1,0:T(8,128)S(1)} %slice_bitcast_fusion.2), channel_id=1, source_target_pairs={{0,32},{32,64},{64,96},{96,128},{128,160},{160,192},{192,224},{1,3... | collective-permute-start | bytes 98312 | tf_op jit(solution)/shard_map/ppermute | solution.py:25
  391.7 234.7 %collective-permute-start.5 = (f32[1,1,64,128]{3,2,1,0:T(8,128)S(1)}, f32[1,1,64,128]{3,2,1,0:T(8,128)S(1)}, u32[]{:S(2)}, u32[]{:S(2)}) collective-permute-start(f32[1,1,64,128]{3,2,1,0:T(8,128)S(1)} %slice_bitcast_fusion.2), channel_id=1, source_target_pairs={{32,0},{64,32},{96,64},{128,96},{160,128},{192,160},{224,192},{33,... | collective-permute-start | bytes 98312 | tf_op jit(solution)/shard_map/ppermute | solution.py:26
  626.5 5.8 collective-permute-start.6
  629.0 5.9 collective-permute-start.7
  673.1 337.7 %copy-start.1 = (f32[256,128]{1,0:T(8,128)}, f32[256,128]{1,0:T(8,128)S(1)}, u32[]{:S(2)}) copy-start(f32[256,128]{1,0:T(8,128)S(1)} %get-tuple-element.44) | copy-start | bytes 393220
  756.3 603.8 %all-reduce.15.cloned.1.call-start = ((), (), s32[]{:S(2)}) async-start(), calls=%async_computation.3 | async-start | bytes 131072 | tf_op jit(solution)/shard_map/psum | solution.py:137
  756.3 238.3 %collective-permute-start.8 = (f32[1,1,64,128]{3,2,1,0:T(8,128)S(1)}, f32[1,1,64,128]{3,2,1,0:T(8,128)S(1)}, u32[]{:S(2)}, u32[]{:S(2)}) collective-permute-start(f32[1,1,64,128]{3,2,1,0:T(8,128)S(1)} %slice_bitcast_fusion.1), channel_id=1, source_target_pairs={{0,32},{32,64},{64,96},{96,128},{128,160},{160,192},{192,224},{1,3... | collective-permute-start | bytes 98312 | tf_op jit(solution)/shard_map/ppermute | solution.py:25
  760.0 234.6 %collective-permute-start.9 = (f32[1,1,64,128]{3,2,1,0:T(8,128)S(1)}, f32[1,1,64,128]{3,2,1,0:T(8,128)S(1)}, u32[]{:S(2)}, u32[]{:S(2)}) collective-permute-start(f32[1,1,64,128]{3,2,1,0:T(8,128)S(1)} %slice_bitcast_fusion.1), channel_id=1, source_target_pairs={{32,0},{64,32},{96,64},{128,96},{160,128},{192,160},{224,192},{33,... | collective-permute-start | bytes 98312 | tf_op jit(solution)/shard_map/ppermute | solution.py:26
  994.7 5.8 collective-permute-start.10
  997.2 5.9 collective-permute-start.11
  1041.3 331.7 %copy-start.21 = (f32[256,128]{1,0:T(8,128)}, f32[256,128]{1,0:T(8,128)S(1)}, u32[]{:S(2)}) copy-start(f32[256,128]{1,0:T(8,128)S(1)} %get-tuple-element.45) | copy-start | bytes 393220
  1126.0 238.4 %collective-permute-start.12 = (f32[1,1,64,128]{3,2,1,0:T(8,128)S(1)}, f32[1,1,64,128]{3,2,1,0:T(8,128)S(1)}, u32[]{:S(2)}, u32[]{:S(2)}) collective-permute-start(f32[1,1,64,128]{3,2,1,0:T(8,128)S(1)} %slice_bitcast_fusion), channel_id=1, source_target_pairs={{0,32},{32,64},{64,96},{96,128},{128,160},{160,192},{192,224},{1,3... | collective-permute-start | bytes 98312 | tf_op jit(solution)/shard_map/ppermute | solution.py:25
  1129.7 234.7 %collective-permute-start.13 = (f32[1,1,64,128]{3,2,1,0:T(8,128)S(1)}, f32[1,1,64,128]{3,2,1,0:T(8,128)S(1)}, u32[]{:S(2)}, u32[]{:S(2)}) collective-permute-start(f32[1,1,64,128]{3,2,1,0:T(8,128)S(1)} %slice_bitcast_fusion), channel_id=1, source_target_pairs={{32,0},{64,32},{96,64},{128,96},{160,128},{192,160},{224,192},{33,... | collective-permute-start | bytes 98312 | tf_op jit(solution)/shard_map/ppermute | solution.py:26
  1364.4 5.8 collective-permute-start.14
  1367.0 5.9 collective-permute-start.15
  (30 other events, 1547.7 us)
Sparse Core Ops, SparseCore 0:
  15.2 243.0 all-reduce.8
  388.1 233.9 all-reduce.10
  756.4 233.8 all-reduce.12
  1126.2 233.8 all-reduce.14
where the time goes:
time: 1510 us; the launch traced here: 1500 us
  waiting for transfers between devices  937 us (62%)
  blocking collectives  305 us (20%)
  local copies, waits for them, and re-layouts  109 us (7%)
  matrix products  73.8 us (5%)
  starting transfers between devices  39.3 us (3%)
  between operations  31.4 us (2%)
    psum x4, waiting for transfers between devices, per_device(): lax.psum(jnp.dot(charges[:, :Q].T, membership, precision=highest), ('gx',...  926 us
    psum x4, blocking collectives, per_device(): margin_values = lax.psum(products, ('gx', 'gy'))  305 us
    gather x16, local copies, waits for them, and re-layouts, class_sum(): gathered = sources[positions[:, d * SLOTS:(d + 1) * SLOTS]]  104 us
    dot_general x16, matrix products, class_sum(): jnp.einsum('ks,ksh->kh', weights[:, d * SLOTS:(d + 1) * SLOTS], gathered,...  38.6 us
  transfers between devices with their start and end apart: 20, of which 8 were waited for; matrix products, arithmetic and copies ran while one was open for 2% of the time, Pallas kernels for 0%

commit v1 on v0

v1 whole, which is shorter than its diff:
```python
import functools
import math

import jax
import jax.numpy as jnp
from jax import lax
from jax.experimental import pallas as pl
from jax.experimental.pallas import tpu as pltpu
from jax.sharding import PartitionSpec as P

MESH = pl.DeviceIdType.MESH
F32 = jnp.float32
BF16 = jnp.bfloat16

LMAX = 10
H = 128
Q = 16
ND = 4
SLOTS = 8
NB = 32
EDGE = 64
ITERS = 4
SPH = 256
NC = 1024
SRC = SPH + 8 * EDGE
LANES = 128
TILES = NC // LANES
AROUND = [(dx, dy) for dx in (-1, 0, 1) for dy in (-1, 0, 1) if (dx, dy) != (0, 0)]
NN = (((1,), (0,)), ((), ()))
NT = (((1,), (1,)), ((), ()))


def spd_mixing(margins):
    order = len(margins)
    diagonal_sum = margins[0][0]
    for a in range(1, order):
        diagonal_sum = diagonal_sum + margins[a][a]
    damping = 0.01 * diagonal_sum / order
    triangle = [[None] * order for a in range(order)]
    for a in range(order):
        for b in range(a + 1):
            running = margins[a][b] + (damping if a == b else 0.0)
            for c in range(b):
                running = running - triangle[a][c] * triangle[b][c]
            if a == b:
                triangle[a][a] = jnp.sqrt(running)
            else:
                triangle[a][b] = running / triangle[b][b]
    forward = []
    for a in range(order):
        running = jnp.ones_like(diagonal_sum)
        for c in range(a):
            running = running - triangle[a][c] * forward[c]
        forward.append(running / triangle[a][a])
    backward = [None] * order
    for a in reversed(range(order)):
        running = forward[a]
        for c in range(a + 1, order):
            running = running - triangle[c][a] * backward[c]
        backward[a] = running / triangle[a][a]
    weight_sum = backward[0]
    for a in range(1, order):
        weight_sum = weight_sum + backward[a]
    return [value / weight_sum for value in backward]


def split(value):
    high = value.astype(BF16)
    return high, (value - high.astype(F32)).astype(BF16)


def dot(a, b, dims=NN):
    return lax.dot_general(a, b, dims, preferred_element_type=F32)


def total(value):
    rows = jnp.sum(value.reshape(-1, 8, LANES), axis=0)
    return jnp.sum(jnp.sum(rows, axis=0, keepdims=True), axis=1, keepdims=True)


def largest(value):
    rows = jnp.max(value.reshape(-1, 8, LANES), axis=0)
    return jnp.max(jnp.max(rows, axis=0, keepdims=True), axis=1, keepdims=True)


def mixed_coefficients(gram):
    zero = jnp.zeros_like(gram[0][0])
    one = jnp.ones_like(zero)
    rhos = [[one] + [zero] * ITERS]
    margins = []
    for t in range(ITERS):
        new = rhos[t]
        image = []
        for l in range(ITERS):
            running = None
            for k in range(t + 1):
                term = new[k] * gram[max(k, l)][min(k, l)]
                running = term if running is None else running + term
            image.append(running)
        row = []
        for a in range(t + 1):
            running = None
            for l in range(a + 1):
                term = rhos[a][l] * image[l]
                running = term if running is None else running + term
            row.append(running)
        margins.append(row)
        full = [[margins[max(a, b)][min(a, b)] for b in range(t + 1)] for a in range(t + 1)]
        mixing = spd_mixing(full)
        following = [zero]
        for k in range(ITERS):
            running = zero
            for a in range(t + 1):
                if k <= a:
                    running = running + mixing[a] * rhos[a][k]
            following.append(running)
        rhos.append(following)
    return rhos[ITERS]


def kernel(
    n_gx,
    n_gy,
    x_hbm,
    solute_ref,
    exposure_ref,
    offset_ref,
    row_ref,
    live_ref,
    coupling_ref,
    cell_ref,
    evaluation_ref,
    projection_ref,
    far_hbm,
    out_ref,
    y,
    far,
    whigh,
    wlow,
    classes,
    member,
    onehot,
    kghigh,
    kglow,
    halo,
    mine,
    part_in,
    plane,
    mid_in,
    whole,
    moments,
    gram_out,
    gram_in,
    gram_mid,
    gram_mid_in,
    load_sem,
    halo_send,
    halo_recv,
    part_send,
    part_recv,
    mid_send,
    mid_recv,
    whole_send,
    whole_recv,
    gram_send,
    gram_recv,
):
    gx = lax.axis_index("gx")
    gy = lax.axis_index("gy")
    piece = LANES // n_gy

    def peer_y(step):
        return (gx, lax.rem(gy + step, n_gy))

    def peer_x(step):
        return (lax.rem(gx + step, n_gx), gy)

    def beside(index):
        dx, dy = AROUND[index]
        return (lax.rem(gx + dx + n_gx, n_gx), lax.rem(gy + dy + n_gy, n_gy))

    barrier = pltpu.get_barrier_semaphore()

    def greet_y(step, carry):
        pl.semaphore_signal(barrier, inc=1, device_id=peer_y(step), device_id_type=MESH)
        return carry

    def greet_x(step, carry):
        pl.semaphore_signal(barrier, inc=1, device_id=peer_x(step), device_id_type=MESH)
        return carry

    load_x = pltpu.make_async_copy(x_hbm, y.at[0], load_sem.at[0])
    load_far = pltpu.make_async_copy(far_hbm, far, load_sem.at[1])
    load_x.start()
    load_far.start()
    lax.fori_loop(1, n_gy, greet_y, 0)
    lax.fori_loop(1, n_gx, greet_x, 0)
    corners = [i for i, (dx, dy) in enumerate(AROUND) if dx != 0 and dy != 0]
    for i in corners:
        pl.semaphore_signal(barrier, inc=1, device_id=beside(i), device_id_type=MESH)

    cell_row = jnp.broadcast_to(cell_ref[...], (LANES, SPH))
    for t in range(TILES):
        cells = lax.broadcasted_iota(jnp.int32, (LANES, SPH), 0) + t * LANES
        member[t * LANES : (t + 1) * LANES, :] = (cell_row == cells).astype(F32).astype(BF16)
    cell_column = cell_row.astype(F32).T
    for t in range(TILES):
        cells = (lax.broadcasted_iota(jnp.int32, (SPH, LANES), 1) + t * LANES).astype(F32)
        onehot[:, t * LANES : (t + 1) * LANES] = (cell_column == cells).astype(F32).astype(BF16)

    def halo_copy(k, index):
        return pltpu.make_async_remote_copy(
            src_ref=y.at[k, pl.ds(0, EDGE)],
            dst_ref=halo.at[k, pl.ds((7 - index) * EDGE, EDGE)],
            send_sem=halo_send.at[k, index],
            recv_sem=halo_recv.at[k, 7 - index],
            device_id=beside(index),
            device_id_type=MESH,
        )

    def part_copy(k, step):
        return pltpu.make_async_remote_copy(
            src_ref=mine.at[k, lax.rem(gy + step, n_gy)],
            dst_ref=part_in.at[k, step],
            send_sem=part_send.at[k],
            recv_sem=part_recv.at[k],
            device_id=peer_y(step),
            device_id_type=MESH,
        )

    def mid_copy(k, step):
        return pltpu.make_async_remote_copy(
            src_ref=plane.at[k],
            dst_ref=mid_in.at[k, step],
            send_sem=mid_send.at[k],
            recv_sem=mid_recv.at[k],
            device_id=peer_x(step),
            device_id_type=MESH,
        )

    def whole_copy(k, step):
        return pltpu.make_async_remote_copy(
            src_ref=whole.at[k, gy],
            dst_ref=whole.at[k, gy],
            send_sem=whole_send.at[k],
            recv_sem=whole_recv.at[k],
            device_id=peer_y(step),
            device_id_type=MESH,
        )

    def gram_copy_y(step):
        return pltpu.make_async_remote_copy(
            src_ref=gram_out.at[0],
            dst_ref=gram_in.at[step],
            send_sem=gram_send.at[0],
            recv_sem=gram_recv.at[0],
            device_id=peer_y(step),
            device_id_type=MESH,
        )

    def gram_copy_x(step):
        return pltpu.make_async_remote_copy(
            src_ref=gram_mid.at[0],
            dst_ref=gram_mid_in.at[step],
            send_sem=gram_send.at[1],
            recv_sem=gram_recv.at[1],
            device_id=peer_x(step),
            device_id_type=MESH,
        )

    def send_all(copy, count):
        def one(step, carry):
            copy(step).start()
            return carry

        lax.fori_loop(1, count, one, 0)

    def bytes_of(ref, sem):
        return pltpu.make_async_copy(ref, ref, sem)

    def begin(k):
        for index in range(8):
            halo_copy(k, index).start()
        first = y[k].T[:Q]
        high, rest = split(first)
        lows = first - high.astype(F32)
        middle, last = split(lows)
        stacked = jnp.concatenate([high, middle, last], axis=0)
        parts = dot(stacked, member[...], NT)
        parts = parts[:Q] + parts[Q : 2 * Q] + parts[2 * Q :]
        per = Q // min(piece, Q)
        for t in range(TILES):
            block = parts[:, t * LANES : (t + 1) * LANES]
            if piece >= Q:
                each = piece // Q
                mine[k, t // each, (t % each) * Q : (t % each + 1) * Q, :] = block
            else:
                for j in range(per):
                    mine[k, t * per + j] = block[j * piece : (j + 1) * piece]
        send_all(functools.partial(part_copy, k), n_gy)

    load_x.wait()
    pl.semaphore_wait(barrier, (n_gy - 1) + (n_gx - 1) + len(corners))
    begin(0)

    block_rows = 16

    def weigh(step, carry):
        base = pl.multiple_of(step * block_rows, block_rows)
        offs = offset_ref[pl.ds(base, block_rows), :]
        owner = row_ref[pl.ds(base, block_rows), :]
        place = jnp.where(
            offs == 4, owner, SPH + jnp.where(offs > 4, offs - 1, offs) * EDGE + owner
        )
        alive = live_ref[pl.ds(base, block_rows), :]
        margin = coupling_ref[pl.ds(base, block_rows), :]
        columns = lax.broadcasted_iota(jnp.int32, (block_rows, SRC), 1)
        for d in range(ND):
            weights = jnp.zeros((block_rows, SRC), F32)
            for s in range(SLOTS):
                slot = d * SLOTS + s
                value = jnp.where(
                    s < alive[:, d : d + 1], margin[:, slot : slot + 1], jnp.float32(0.0)
                )
                weights = weights + jnp.where(
                    place[:, slot : slot + 1] == columns, value, jnp.float32(0.0)
                )
            high, low = split(weights)
            rows = pl.ds(pl.multiple_of(d * SPH + base, block_rows), block_rows)
            whigh[rows, :] = high
            wlow[rows, :] = low
        return carry

    lax.fori_loop(0, SPH // block_rows, weigh, 0)

    load_far.wait()
    for t in range(TILES):
        high, low = split(far[t * LANES : (t + 1) * LANES, :])
        kghigh[:, t * LANES : (t + 1) * LANES] = dot(onehot[...], high, NT).astype(BF16)
        kglow[:, t * LANES : (t + 1) * LANES] = dot(onehot[...], low, NT).astype(BF16)

    index = lax.broadcasted_iota(jnp.int32, (1, H), 1)
    degree = jnp.zeros((1, H), F32)
    for n in range(1, LMAX + 1):
        degree = degree + (index >= n * n).astype(F32)
    scale = jnp.where(index < (LMAX + 1) ** 2, (2.0 * degree + 1.0) / (4.0 * math.pi), 0.0)
    evaluation_parts = jnp.concatenate(split(evaluation_ref[...]), axis=1)
    projection_parts = jnp.concatenate(split(projection_ref[...]), axis=1)

    def product(left, right):
        high, low = split(left)
        both = dot(high, right)
        return both[:, :H] + both[:, H:] + dot(low, right[:, :H])

    def near_part(d, columns, source):
        rows = pl.ds(d * SPH, SPH)
        both = dot(whigh[rows, columns], source)
        return both[:, :H] + both[:, H:] + dot(wlow[rows, columns], source[:, :H])

    def iterate(k, carry):
        own = jnp.concatenate(split(y[k]), axis=1)
        for d in range(ND):
            classes[:, d * H : (d + 1) * H] = near_part(d, pl.ds(0, SPH), own)

        bytes_of(part_in.at[k, pl.ds(1, n_gy - 1)], part_recv.at[k]).wait()
        plane[k] = jnp.sum(part_in[k, 1:], axis=0) + mine[k, gy]
        send_all(functools.partial(mid_copy, k), n_gx)

        for i in range(8):
            halo_copy(k, i).wait_recv()
        others = jnp.concatenate(split(halo[k]), axis=1)
        for d in range(ND):
            classes[:, d * H : (d + 1) * H] += near_part(d, pl.ds(SPH, 8 * EDGE), others)

        bytes_of(mid_in.at[k, pl.ds(1, n_gx - 1)], mid_recv.at[k]).wait()
        whole[k, gy] = jnp.sum(mid_in[k, 1:], axis=0) + plane[k]
        send_all(functools.partial(whole_copy, k), n_gy)

        potential = product(classes[...], evaluation_parts)
        nearby = product(potential * exposure_ref[...], projection_parts)
        near = solute_ref[...] - nearby

        bytes_of(whole.at[k, pl.ds(0, n_gy - 1)], whole_recv.at[k]).wait()
        for t in range(TILES):
            columns = slice(t * LANES, (t + 1) * LANES)
            if piece >= Q:
                each = piece // Q
                moments[:, columns] = whole[k, t // each, (t % each) * Q : (t % each + 1) * Q, :]
            else:
                per = Q // piece
                for j in range(per):
                    moments[j * piece : (j + 1) * piece, columns] = whole[k, t * per + j]
        high, low = split(moments[...])
        blank = jnp.zeros((H - Q, NC), BF16)
        both = jnp.concatenate([high, blank, low, blank], axis=0)
        far_both = dot(kghigh[...], both, NT)
        distant = far_both[:, :H] + far_both[:, H:] + dot(kglow[...], both[:H], NT)
        y[k + 1] = scale * (near - distant)

        @pl.when(k < ITERS - 1)
        def _():
            begin(k + 1)

        for i in range(8):
            halo_copy(k, i).wait_send()
        sent = pl.ds(0, n_gy - 1)
        bytes_of(mine.at[k, sent], part_send.at[k]).wait()
        bytes_of(mid_in.at[k, pl.ds(1, n_gx - 1)], mid_send.at[k]).wait()
        bytes_of(whole.at[k, sent], whole_send.at[k]).wait()
        return carry

    lax.fori_loop(0, ITERS, iterate, 0)

    changes = [y[k + 1] - y[k] for k in range(ITERS)]
    height = jnp.abs(changes[0])
    for k in range(1, ITERS):
        height = jnp.maximum(height, jnp.abs(changes[k]))
    top = largest(height)
    top = jnp.where(top > 0.0, top, 1.0)
    inverse = 1.0 / top
    changes = [change * inverse for change in changes]
    lane = lax.broadcasted_iota(jnp.int32, (1, LANES), 1)
    pairs = [(a, b) for a in range(ITERS) for b in range(a + 1)]
    line = jnp.where(lane == len(pairs), top, 0.0)
    for i, (a, b) in enumerate(pairs):
        line = line + jnp.where(lane == i, total(changes[a] * changes[b]), 0.0)

    def merged(lines):
        tops = lines[:, len(pairs) : len(pairs) + 1]
        most = jnp.max(tops, axis=0, keepdims=True)
        ratio = tops / most
        sums = jnp.sum(lines * (ratio * ratio), axis=0, keepdims=True)
        return jnp.where(lane == len(pairs), most, sums)

    gram_out[0] = line
    gram_in[0] = line
    send_all(gram_copy_y, n_gy)
    bytes_of(gram_in.at[pl.ds(1, n_gy - 1)], gram_recv.at[0]).wait()
    line = merged(gram_in[...].reshape(n_gy, LANES))
    gram_mid[0] = line
    gram_mid_in[0] = line
    send_all(gram_copy_x, n_gx)
    bytes_of(gram_mid_in.at[pl.ds(1, n_gx - 1)], gram_recv.at[1]).wait()
    line = merged(gram_mid_in[...].reshape(n_gx, LANES))

    gram = [[None] * ITERS for a in range(ITERS)]
    for i, (a, b) in enumerate(pairs):
        gram[a][b] = line[:, i : i + 1]
    rho = mixed_coefficients(gram)
    mixed = rho[1] * y[1]
    for k in range(2, ITERS + 1):
        mixed = mixed + rho[k] * y[k]
    out_ref[...] = mixed

    bytes_of(gram_in.at[pl.ds(1, n_gy - 1)], gram_send.at[0]).wait()
    bytes_of(gram_mid_in.at[pl.ds(1, n_gx - 1)], gram_send.at[1]).wait()


def per_device(
    n_gx,
    n_gy,
    start_charges,
    solute_field,
    exposure,
    owner_offset,
    owner_row,
    live_slots,
    coupling,
    cell_index,
    evaluation,
    projection,
    far_kernel,
):
    vmem = pl.BlockSpec(memory_space=pltpu.VMEM)
    hbm = pl.BlockSpec(memory_space=pl.ANY)
    piece = LANES // n_gy
    dma = pltpu.SemaphoreType.DMA
    return pl.pallas_call(
        functools.partial(kernel, n_gx, n_gy),
        out_shape=jax.ShapeDtypeStruct((SPH, H), F32),
        in_specs=[hbm] + [vmem] * 9 + [hbm],
        out_specs=vmem,
        scratch_shapes=[
            pltpu.VMEM((ITERS + 1, SPH, H), F32),
            pltpu.VMEM((NC, NC), F32),
            pltpu.VMEM((ND * SPH, SRC), BF16),
            pltpu.VMEM((ND * SPH, SRC), BF16),
            pltpu.VMEM((SPH, ND * H), F32),
            pltpu.VMEM((NC, SPH), BF16),
            pltpu.VMEM((SPH, NC), BF16),
            pltpu.VMEM((SPH, NC), BF16),
            pltpu.VMEM((SPH, NC), BF16),
            pltpu.VMEM((ITERS, 8 * EDGE, H), F32),
            pltpu.VMEM((ITERS, n_gy, piece, LANES), F32),
            pltpu.VMEM((ITERS, n_gy, piece, LANES), F32),
            pltpu.VMEM((ITERS, piece, LANES), F32),
            pltpu.VMEM((ITERS, n_gx, piece, LANES), F32),
            pltpu.VMEM((ITERS, n_gy, piece, LANES), F32),
            pltpu.VMEM((Q, NC), F32),
            pltpu.VMEM((1, 1, LANES), F32),
            pltpu.VMEM((n_gy, 1, LANES), F32),
            pltpu.VMEM((1, 1, LANES), F32),
            pltpu.VMEM((n_gx, 1, LANES), F32),
            dma((2,)),
            dma((ITERS, 8)),
            dma((ITERS, 8)),
            dma((ITERS,)),
            dma((ITERS,)),
            dma((ITERS,)),
            dma((ITERS,)),
            dma((ITERS,)),
            dma((ITERS,)),
            dma((2,)),
            dma((2,)),
        ],
        compiler_params=pltpu.CompilerParams(
            collective_id=0, has_side_effects=True, vmem_limit_bytes=48 * 1024 * 1024
        ),
        name="screening",
    )(
        start_charges,
        solute_field,
        exposure,
        owner_offset,
        owner_row,
        live_slots,
        coupling,
        cell_index.reshape(1, SPH),
        evaluation,
        projection,
        far_kernel,
    )


def solution(mesh):
    placed = (
        P(("gx", "gy"), None),
        P(("gx", "gy"), None),
        P(("gx", "gy"), None),
        P(("gx", "gy"), None),
        P(("gx", "gy"), None),
        P(("gx", "gy"), None),
        P(("gx", "gy"), None),
        P(("gx", "gy")),
        P(),
        P(),
        P(),
    )
    return jax.shard_map(
        functools.partial(per_device, mesh.shape["gx"], mesh.shape["gy"]),
        mesh=mesh,
        in_specs=placed,
        out_specs=P(("gx", "gy"), None),
        check_vma=False,
    )
```

time: 1510 us -> 111 us (0.07)
  waiting for transfers between devices: 937 us -> 0 us
  blocking collectives: 305 us -> 0 us
  Pallas kernels: 0 us -> 99.5 us
  local copies, waits for them, and re-layouts: 109 us -> 11.4 us
  matrix products: 73.8 us -> 0 us
  starting transfers between devices: 39.3 us -> 0 us
  between operations: 31.4 us -> 0.03 us
    psum x4 -> x0, waiting for transfers between devices: 926 us -> none  [per_device(): lax.psum(jnp.dot(charges[:, :Q].T, membership, precision=highest), ('gx',...]
    psum x4 -> x0, blocking collectives: 305 us -> none  [per_device(): margin_values = lax.psum(products, ('gx', 'gy'))]
    gather x16 -> x0, local copies, waits for them, and re-layouts: 104 us -> none  [class_sum(): gathered = sources[positions[:, d * SLOTS:(d + 1) * SLOTS]]]
    pallas_call x0 -> x1, Pallas kernels: none -> 99.5 us  [per_device(): pl.pallas_call(functools.partial(kernel, n_gx, n_gy), out_shape=jax.Shape...]
    dot_general x36 -> x0, matrix products: 73.8 us -> none  [the longest x16 38.6 us: class_sum(): jnp.einsum('ks,ksh->kh', weights[:, d * SLOTS:(d + 1) * SLOTS], gathered,...]
    ppermute x16 -> x0, starting transfers between devices: 39.2 us -> none  [the longest x8 25.6 us: padded(): before = lax.ppermute(last, axis, up)]
  transfers between devices with their start and end apart: 20 -> 0, of which waited for: 8 -> 0; matrix products, arithmetic and copies ran while one was open for 2% -> 0% of each run, Pallas kernels for 0% -> 0%
where the time goes in v1:
time: 111 us
  Pallas kernels  99.5 us (90%)
  local copies, waits for them, and re-layouts  11.4 us (10%)
    pallas_call x1, Pallas kernels, per_device(): pl.pallas_call(functools.partial(kernel, n_gx, n_gy), out_shape=jax.Shape...  99.5 us
    unnamed x19, local copies, waits for them, and re-layouts  11.4 us

profile of v1, /device:TPU:1, one launch (start us, length us, event | category | flops | bytes accessed | tf_op | source)
XLA Modules:
  0.0 111.0 jit_solution(8984937219220571011)
XLA Ops:
  0.0 0.9 copy.12.offset_ref
  0.9 0.9 copy.13.row_ref
  1.7 0.8 copy.14.live_ref
  2.5 0.9 copy.15.coupling_ref
  3.4 0.0 copy-start
  3.4 2.2 %copy-done = f32[1024,1024]{1,0:T(8,128)S(1)} copy-done((f32[1024,1024]{1,0:T(8,128)S(1)}, f32[1024,1024]{1,0:T(8,128)}, u32[]{:S(2)}) %copy-start) | copy-done | bytes 4194328
  5.6 0.0 copy-start.1
  5.6 0.9 copy-done.1
  6.5 0.0 copy-start.2
  6.5 0.9 copy-done.2
  7.4 0.0 copy-start.3
  7.4 0.9 copy-done.3
  8.3 0.0 copy-start.4
  8.4 0.9 copy-done.4
  9.3 0.0 copy-start.5
  9.3 0.8 copy-done.5
  10.1 0.0 copy-start.6
  10.1 0.7 copy-done.6
  10.8 99.5 %screening.1 = f32[256,128]{1,0:T(8,128)S(1)} custom-call(f32[256,128]{1,0:T(8,128)S(1)} %copy-done.2, f32[256,128]{1,0:T(8,128)S(1)} %copy-done.3, f32[256,128]{1,0:T(8,128)S(1)} %copy-done.4, s32[256,32]{1,0:T(8,128)S(1)} %copy.12.offset_ref, s32[256,32]{1,0:T(8,128)S(1)} %copy.13.row_ref, s32[256,4]{1,0:T(8,128)S(1)} %copy.14.live_ref, ...), custom_call_target="tpu_custom_call" | custom-call | tf_op jit(solution)/shard_map/screening/pallas_call | solution.py:478
  110.3 0.7 copy.17
Async XLA Ops:
  3.4 2.2 %copy-start = (f32[1024,1024]{1,0:T(8,128)S(1)}, f32[1024,1024]{1,0:T(8,128)}, u32[]{:S(2)}) copy-start(f32[1024,1024]{1,0:T(8,128)} %far_hbm.1) | copy-start | bytes 12582916
  5.6 0.9 copy-start.1
  6.5 0.9 copy-start.2
  7.4 0.9 copy-start.3
  8.3 0.9 copy-start.4
  9.3 0.8 copy-start.5
  10.1 0.7 copy-start.6

commit v2 on v1

v2 whole, which is shorter than its diff:
```python
import functools
import math

import jax
import jax.numpy as jnp
from jax import lax
from jax.experimental import pallas as pl
from jax.experimental.pallas import tpu as pltpu
from jax.sharding import PartitionSpec as P

MESH = pl.DeviceIdType.MESH
F32 = jnp.float32
BF16 = jnp.bfloat16

LMAX = 10
H = 128
Q = 16
ND = 4
SLOTS = 8
NB = 32
EDGE = 64
ITERS = 4
SPH = 256
NC = 1024
SRC = SPH + 8 * EDGE
LANES = 128
TILES = NC // LANES
AROUND = [(dx, dy) for dx in (-1, 0, 1) for dy in (-1, 0, 1) if (dx, dy) != (0, 0)]
NN = (((1,), (0,)), ((), ()))
NT = (((1,), (1,)), ((), ()))


def spd_mixing(margins):
    order = len(margins)
    diagonal_sum = margins[0][0]
    for a in range(1, order):
        diagonal_sum = diagonal_sum + margins[a][a]
    damping = 0.01 * diagonal_sum / order
    triangle = [[None] * order for a in range(order)]
    for a in range(order):
        for b in range(a + 1):
            running = margins[a][b] + (damping if a == b else 0.0)
            for c in range(b):
                running = running - triangle[a][c] * triangle[b][c]
            if a == b:
                triangle[a][a] = jnp.sqrt(running)
            else:
                triangle[a][b] = running / triangle[b][b]
    forward = []
    for a in range(order):
        running = jnp.ones_like(diagonal_sum)
        for c in range(a):
            running = running - triangle[a][c] * forward[c]
        forward.append(running / triangle[a][a])
    backward = [None] * order
    for a in reversed(range(order)):
        running = forward[a]
        for c in range(a + 1, order):
            running = running - triangle[c][a] * backward[c]
        backward[a] = running / triangle[a][a]
    weight_sum = backward[0]
    for a in range(1, order):
        weight_sum = weight_sum + backward[a]
    return [value / weight_sum for value in backward]


def split(value):
    high = value.astype(BF16)
    return high, (value - high.astype(F32)).astype(BF16)


def dot(a, b, dims=NN):
    return lax.dot_general(a, b, dims, preferred_element_type=F32)


def total(value):
    rows = jnp.sum(value.reshape(-1, 8, LANES), axis=0)
    return jnp.sum(jnp.sum(rows, axis=0, keepdims=True), axis=1, keepdims=True)


def largest(value):
    rows = jnp.max(value.reshape(-1, 8, LANES), axis=0)
    return jnp.max(jnp.max(rows, axis=0, keepdims=True), axis=1, keepdims=True)


def mixed_coefficients(gram):
    zero = jnp.zeros_like(gram[0][0])
    one = jnp.ones_like(zero)
    rhos = [[one] + [zero] * ITERS]
    margins = []
    for t in range(ITERS):
        new = rhos[t]
        image = []
        for l in range(ITERS):
            running = None
            for k in range(t + 1):
                term = new[k] * gram[max(k, l)][min(k, l)]
                running = term if running is None else running + term
            image.append(running)
        row = []
        for a in range(t + 1):
            running = None
            for l in range(a + 1):
                term = rhos[a][l] * image[l]
                running = term if running is None else running + term
            row.append(running)
        margins.append(row)
        full = [[margins[max(a, b)][min(a, b)] for b in range(t + 1)] for a in range(t + 1)]
        mixing = spd_mixing(full)
        following = [zero]
        for k in range(ITERS):
            running = zero
            for a in range(t + 1):
                if k <= a:
                    running = running + mixing[a] * rhos[a][k]
            following.append(running)
        rhos.append(following)
    return rhos[ITERS]


def kernel(
    n_gx,
    n_gy,
    x_hbm,
    solute_hbm,
    exposure_hbm,
    offset_hbm,
    row_hbm,
    live_hbm,
    coupling_hbm,
    cell_hbm,
    evaluation_hbm,
    projection_hbm,
    far_hbm,
    out_ref,
    solute,
    exposure,
    offset,
    row,
    live,
    coupling,
    cell,
    evaluation,
    projection,
    far,
    y,
    z,
    slots,
    whigh,
    wlow,
    source,
    member,
    onehot,
    farhigh,
    farlow,
    kghigh,
    kglow,
    near_cells,
    halo,
    mine,
    part_in,
    plane,
    mid_in,
    whole,
    moments,
    counts,
    scaled,
    expanded,
    unit,
    gram_out,
    gram_in,
    load_sem,
    halo_send,
    halo_recv,
    cell_send,
    cell_recv,
    part_send,
    part_recv,
    mid_send,
    mid_recv,
    whole_send,
    whole_recv,
    gram_send,
    gram_recv,
):
    gx = lax.axis_index("gx")
    gy = lax.axis_index("gy")
    piece = LANES // n_gy

    def peer_y(step):
        return (gx, lax.rem(gy + step, n_gy))

    def peer_x(step):
        return (lax.rem(gx + step, n_gx), gy)

    def beside(index):
        dx, dy = AROUND[index]
        return (lax.rem(gx + dx + n_gx, n_gx), lax.rem(gy + dy + n_gy, n_gy))

    def greet(device):
        pl.semaphore_signal(barrier, inc=1, device_id=device, device_id_type=MESH)

    def each(first, last, act):
        def one(step, carry):
            act(step)
            return carry

        lax.fori_loop(first, last, one, 0)

    loads = [
        pltpu.make_async_copy(there, here, load_sem.at[i])
        for i, (there, here) in enumerate(
            [
                (cell_hbm, cell),
                (offset_hbm, offset),
                (row_hbm, row),
                (live_hbm, live),
                (coupling_hbm, coupling),
                (x_hbm, z.at[0]),
                (x_hbm, y.at[0]),
                (far_hbm, far),
                (evaluation_hbm, evaluation),
                (exposure_hbm, exposure),
                (projection_hbm, projection),
                (solute_hbm, solute),
            ]
        )
    ]
    for load in loads:
        load.start()
    barrier = pltpu.get_barrier_semaphore()
    each(1, n_gy, lambda step: greet(peer_y(step)))
    each(1, n_gx, lambda step: greet(peer_x(step)))
    corners = [i for i, (dx, dy) in enumerate(AROUND) if dx != 0 and dy != 0]
    for i in corners:
        greet(beside(i))

    def bytes_of(ref, sem):
        return pltpu.make_async_copy(ref, ref, sem)

    def halo_copy(k, index):
        return pltpu.make_async_remote_copy(
            src_ref=z.at[k, pl.ds(0, EDGE)],
            dst_ref=halo.at[k, pl.ds((7 - index) * EDGE, EDGE)],
            send_sem=halo_send.at[k, index],
            recv_sem=halo_recv.at[k, 7 - index],
            device_id=beside(index),
            device_id_type=MESH,
        )

    def cell_copy(index):
        return pltpu.make_async_remote_copy(
            src_ref=near_cells.at[8],
            dst_ref=near_cells.at[7 - index],
            send_sem=cell_send.at[index],
            recv_sem=cell_recv.at[7 - index],
            device_id=beside(index),
            device_id_type=MESH,
        )

    def part_copy(k, step):
        return pltpu.make_async_remote_copy(
            src_ref=mine.at[k, lax.rem(gy + step, n_gy)],
            dst_ref=part_in.at[k, step],
            send_sem=part_send.at[k],
            recv_sem=part_recv.at[k],
            device_id=peer_y(step),
            device_id_type=MESH,
        )

    def mid_copy(k, step):
        return pltpu.make_async_remote_copy(
            src_ref=plane.at[k],
            dst_ref=mid_in.at[k, step],
            send_sem=mid_send.at[k],
            recv_sem=mid_recv.at[k],
            device_id=peer_x(step),
            device_id_type=MESH,
        )

    def whole_copy(k, step):
        return pltpu.make_async_remote_copy(
            src_ref=whole.at[k, gy],
            dst_ref=whole.at[k, gy],
            send_sem=whole_send.at[k],
            recv_sem=whole_recv.at[k],
            device_id=peer_y(step),
            device_id_type=MESH,
        )

    def gram_copy(step):
        return pltpu.make_async_remote_copy(
            src_ref=gram_out.at[0],
            dst_ref=gram_in.at[step],
            send_sem=gram_send.at[0],
            recv_sem=gram_recv.at[0],
            device_id=(lax.rem(gx + step // n_gy, n_gx), lax.rem(gy + step % n_gy, n_gy)),
            device_id_type=MESH,
        )

    def prepare(k):
        first = z[k].T[:Q]
        high, rest = split(first)
        middle, last = split(first - high.astype(F32))
        ones = jnp.ones((Q, SPH), BF16)
        stacked = jnp.concatenate([high, middle, last, ones], axis=0)
        parts = dot(stacked, member[...], NT)
        number = parts[3 * Q : 3 * Q + 1]
        parts = parts[:Q] + parts[Q : 2 * Q] + parts[2 * Q : 3 * Q]
        for t in range(TILES):
            columns = slice(t * LANES, (t + 1) * LANES)
            if piece >= Q:
                fold = piece // Q
                mine[k, t // fold, (t % fold) * Q : (t % fold + 1) * Q, :] = parts[:, columns]
                at = piece + t % fold
                mine[k, t // fold, at : at + 1, :] = number[:, columns]
            else:
                per = Q // piece
                for j in range(per):
                    mine[k, t * per + j, :piece, :] = parts[j * piece : (j + 1) * piece, columns]
                    mine[k, t * per + j, piece : piece + 1, :] = number[:, columns]

    def send_halo(k):
        for index in range(8):
            halo_copy(k, index).start()

    def send_part(k):
        each(1, n_gy, functools.partial(lambda k, step: part_copy(k, step).start(), k))

    def pass_on(k):
        bytes_of(part_in.at[k, pl.ds(1, n_gy - 1)], part_recv.at[k]).wait()
        plane[k] = jnp.sum(part_in[k, 1:], axis=0) + mine[k, gy]
        each(1, n_gx, lambda step: mid_copy(k, step).start())

    def spread(k):
        bytes_of(mid_in.at[k, pl.ds(1, n_gx - 1)], mid_recv.at[k]).wait()
        whole[k, gy] = jnp.sum(mid_in[k, 1:], axis=0) + plane[k]
        each(1, n_gy, lambda step: whole_copy(k, step).start())

    index = lax.broadcasted_iota(jnp.int32, (1, H), 1)
    degree = jnp.zeros((1, H), F32)
    for n in range(1, LMAX + 1):
        degree = degree + (index >= n * n).astype(F32)
    scale = jnp.where(index < (LMAX + 1) ** 2, (2.0 * degree + 1.0) / (4.0 * math.pi), 0.0)
    component = lax.broadcasted_iota(jnp.int32, (Q, NC), 0)
    moment_degree = jnp.zeros((Q, NC), F32)
    for n in range(1, 4):
        moment_degree = moment_degree + (component >= n * n).astype(F32)
    moment_scale = (2.0 * moment_degree + 1.0) / (4.0 * math.pi)

    def gathered(k):
        bytes_of(whole.at[k, pl.ds(0, n_gy - 1)], whole_recv.at[k]).wait()
        for t in range(TILES):
            columns = slice(t * LANES, (t + 1) * LANES)
            if piece >= Q:
                fold = piece // Q
                moments[:, columns] = whole[k, t // fold, (t % fold) * Q : (t % fold + 1) * Q, :]
                at = piece + t % fold
                counts[:, columns] = whole[k, t // fold, at : at + 1, :]
            else:
                per = Q // piece
                for j in range(per):
                    moments[j * piece : (j + 1) * piece, columns] = whole[k, t * per + j, :piece, :]
                counts[:, columns] = whole[k, t * per, piece : piece + 1, :]
        value = moment_scale * (moments[...] - counts[...] * expanded[...])
        scaled[...] = value
        high, low = split(value)
        blank = jnp.zeros((H - Q, NC), BF16)
        return jnp.concatenate([high, blank, low, blank], axis=0)

    def distant(both, rows):
        result = dot(kghigh[rows, :], both, NT)
        return result[:, :H] + result[:, H:] + dot(kglow[rows, :], both[:H], NT)

    def expand():
        high, low = split(scaled[...])
        both = dot(jnp.concatenate([high, low], axis=0), farhigh[...])
        expanded[...] = both[:Q] + both[Q:] + dot(high, farlow[...])

    def far_rows(at, first_cells, second_cells):
        cells = jnp.concatenate(
            [
                jnp.broadcast_to(first_cells, (LANES, LANES)).T,
                jnp.broadcast_to(second_cells, (LANES, LANES)).T,
            ],
            axis=0,
        )
        for t in range(TILES):
            numbers = lax.broadcasted_iota(jnp.int32, (SPH, LANES), 1) + t * LANES
            columns = slice(t * LANES, (t + 1) * LANES)
            onehot[:, columns] = (cells == numbers.astype(F32)).astype(F32).astype(BF16)
        rows = slice(at, at + SPH)

        def one(step):
            block = pl.ds(pl.multiple_of(step * SPH, SPH), SPH)
            kghigh[rows, block] = dot(onehot[...], farhigh[block, :], NT).astype(BF16)
            kglow[rows, block] = dot(onehot[...], farlow[block, :], NT).astype(BF16)

        each(0, NC // SPH, one)

    loads[0].wait()
    cell_row = jnp.broadcast_to(cell[...], (LANES, SPH))
    for t in range(TILES):
        cells = lax.broadcasted_iota(jnp.int32, (LANES, SPH), 0) + t * LANES
        member[t * LANES : (t + 1) * LANES, :] = (cell_row == cells).astype(F32).astype(BF16)
    own_cells = cell[...].astype(F32)
    near_cells[8] = jnp.concatenate([own_cells[:, :EDGE], own_cells[:, :EDGE]], axis=1)

    for i in range(1, 5):
        loads[i].wait()
    offsets = offset[...]
    place = jnp.where(
        offsets == 4,
        row[...],
        SPH + jnp.where(offsets > 4, offsets - 1, offsets) * EDGE + row[...],
    )
    alive = jnp.concatenate(
        [jnp.broadcast_to(live[d : d + 1, :], (SLOTS, SPH)) for d in range(ND)], axis=0
    )
    slot = lax.broadcasted_iota(jnp.int32, (NB, SPH), 0) & (SLOTS - 1)
    weights = jnp.where(slot < alive, coupling[...], 0.0)
    blank = jnp.zeros((LANES - 2 * NB, SPH), F32)
    slots[...] = jnp.concatenate([place.astype(F32), weights, blank], axis=0).T

    block_rows = 16

    def weigh(step):
        base = pl.multiple_of(step * block_rows, block_rows)
        held = slots[pl.ds(base, block_rows), :]
        lanes = lax.broadcasted_iota(jnp.int32, (block_rows, LANES), 1).astype(F32)
        for d in range(ND):
            sums = [jnp.zeros((block_rows, LANES), F32) for t in range(SRC // LANES)]
            for s in range(d * SLOTS, (d + 1) * SLOTS):
                where = jnp.broadcast_to(held[:, s : s + 1], (block_rows, LANES))
                value = jnp.broadcast_to(held[:, NB + s : NB + s + 1], (block_rows, LANES))
                for t in range(SRC // LANES):
                    sums[t] = sums[t] + jnp.where(where == lanes + t * LANES, value, 0.0)
            high, low = split(jnp.concatenate(sums, axis=1))
            rows = pl.ds(pl.multiple_of(d * SPH + base, block_rows), block_rows)
            whigh[rows, :] = high
            wlow[rows, :] = low

    each(0, SPH // block_rows, weigh)

    loads[5].wait()
    prepare(0)
    pl.semaphore_wait(barrier, (n_gy - 1) + (n_gx - 1) + len(corners))
    send_halo(0)
    for i in range(8):
        cell_copy(i).start()
    send_part(0)

    loads[7].wait()
    for t in range(TILES):
        rows = slice(t * LANES, (t + 1) * LANES)
        high, low = split(far[rows, :])
        farhigh[rows, :] = high
        farlow[rows, :] = low
    far_rows(0, own_cells[:, :LANES], own_cells[:, LANES:])
    expanded[...] = jnp.zeros_like(expanded)
    for load in loads[8:] + loads[6:7]:
        load.wait()
    evaluation_parts = jnp.concatenate(split(evaluation[...]), axis=1)
    projection_parts = jnp.concatenate(split(projection[...]), axis=1)
    lane = lax.broadcasted_iota(jnp.int32, (1, LANES), 1)

    def product(left, right):
        high, low = split(left)
        both = dot(high, right)
        return both[:, :H] + both[:, H:] + dot(low, right[:, :H])

    def neighbour_cells(pair):
        return jnp.where(lane < EDGE, near_cells[2 * pair], near_cells[2 * pair + 1])

    def put(rows, value):
        high, low = split(value)
        source[rows, :H] = high
        source[rows, H:] = low

    def iterate(k, carry):
        @pl.when(k == 1)
        def _():
            for i in range(8):
                cell_copy(i).wait_recv()
            far_rows(SPH, neighbour_cells(0), neighbour_cells(1))

        @pl.when(k > 0)
        def _():
            spread(k - 1)

        @pl.when(k == 1)
        def _():
            far_rows(2 * SPH, neighbour_cells(2), neighbour_cells(3))

        pass_on(k)

        for i in range(8):
            halo_copy(k, i).wait_recv()

        @pl.when(k == 0)
        def _():
            put(slice(0, SPH), y[0])
            put(slice(SPH, SRC), halo[0])

        @pl.when(k > 0)
        def _():
            taken = distant(gathered(k - 1), slice(0, SRC))
            own = z[k] - taken[:SPH]
            y[k] = own
            put(slice(0, SPH), own)
            put(slice(SPH, SRC), halo[k] - taken[SPH:])

        potential = jnp.zeros((SPH, H), F32)
        for d in range(ND):
            rows = slice(d * SPH, (d + 1) * SPH)
            both = dot(whigh[rows, :], source[...])
            sums = both[:, :H] + both[:, H:] + dot(wlow[rows, :], source[:, :H])
            potential = potential + product(sums, evaluation_parts[d * H : (d + 1) * H])
        nearby = product(potential * exposure[...], projection_parts)
        z[k + 1] = scale * (solute[...] - nearby)

        @pl.when(k < ITERS - 1)
        def _():
            send_halo(k + 1)
            prepare(k + 1)
            send_part(k + 1)

        @pl.when(k > 0)
        def _():
            expand()

        return carry

    lax.fori_loop(0, ITERS, iterate, 0)

    spread(ITERS - 1)
    pairs = [(a, b) for a in range(ITERS) for b in range(a + 1)]
    early = [y[k + 1] - y[k] for k in range(ITERS - 1)]
    height = jnp.abs(early[0])
    for change in early[1:]:
        height = jnp.maximum(height, jnp.abs(change))
    top = largest(height)
    top = jnp.where(top > 0.0, top, 1.0)
    inverse = 1.0 / top
    for k in range(ITERS - 1):
        unit[k] = early[k] * inverse
    line = jnp.zeros((1, LANES), F32)
    for i, (a, b) in enumerate(pairs):
        if a < ITERS - 1:
            line = line + jnp.where(lane == i, total(unit[a] * unit[b]), 0.0)

    last = z[ITERS] - distant(gathered(ITERS - 1), slice(0, SPH))
    y[ITERS] = last
    change = last - y[ITERS - 1]
    most = jnp.maximum(top, largest(jnp.abs(change)))
    ratio = top / most
    change = change * (1.0 / most)
    line = line * (ratio * ratio)
    for i, (a, b) in enumerate(pairs):
        if a == ITERS - 1:
            sums = total(change * change) if b == a else total(change * unit[b]) * ratio
            line = line + jnp.where(lane == i, sums, 0.0)
    line = jnp.where(lane == len(pairs), most, line)
    gram_out[0] = line
    gram_in[0] = line
    everyone = n_gx * n_gy
    each(1, everyone, lambda step: gram_copy(step).start())
    bytes_of(gram_in.at[pl.ds(1, everyone - 1)], gram_recv.at[0]).wait()
    lines = gram_in[...].reshape(everyone, LANES)
    tops = lines[:, len(pairs) : len(pairs) + 1]
    ratio = tops / jnp.max(tops, axis=0, keepdims=True)
    line = jnp.sum(lines * (ratio * ratio), axis=0, keepdims=True)

    gram = [[None] * ITERS for a in range(ITERS)]
    for i, (a, b) in enumerate(pairs):
        gram[a][b] = line[:, i : i + 1]
    rho = mixed_coefficients(gram)
    mixed = rho[1] * y[1]
    for k in range(2, ITERS + 1):
        mixed = mixed + rho[k] * y[k]
    out_ref[...] = mixed

    def sent(k):
        for i in range(8):
            halo_copy(k, i).wait_send()
        peers = pl.ds(0, n_gy - 1)
        bytes_of(mine.at[k, peers], part_send.at[k]).wait()
        bytes_of(mid_in.at[k, pl.ds(1, n_gx - 1)], mid_send.at[k]).wait()
        bytes_of(whole.at[k, peers], whole_send.at[k]).wait()

    each(0, ITERS, sent)
    for i in range(8):
        cell_copy(i).wait_send()
    bytes_of(gram_in.at[pl.ds(1, everyone - 1)], gram_send.at[0]).wait()


def per_device(
    n_gx,
    n_gy,
    start_charges,
    solute_field,
    exposure,
    owner_offset,
    owner_row,
    live_slots,
    coupling,
    cell_index,
    evaluation,
    projection,
    far_kernel,
):
    hbm = pl.BlockSpec(memory_space=pl.ANY)
    piece = LANES // n_gy
    rows = piece + max(1, piece // Q)
    dma = pltpu.SemaphoreType.DMA

    def held(*shape, dtype=F32):
        return pltpu.VMEM(shape, dtype)

    return pl.pallas_call(
        functools.partial(kernel, n_gx, n_gy),
        out_shape=jax.ShapeDtypeStruct((SPH, H), F32),
        in_specs=[hbm] * 11,
        out_specs=pl.BlockSpec(memory_space=pltpu.VMEM),
        scratch_shapes=[
            held(SPH, H),
            held(SPH, H),
            held(NB, SPH, dtype=jnp.int32),
            held(NB, SPH, dtype=jnp.int32),
            held(ND, SPH, dtype=jnp.int32),
            held(NB, SPH),
            held(1, SPH, dtype=jnp.int32),
            held(ND * H, H),
            held(H, H),
            held(NC, NC),
            held(ITERS + 1, SPH, H),
            held(ITERS + 1, SPH, H),
            held(SPH, LANES),
            held(ND * SPH, SRC, dtype=BF16),
            held(ND * SPH, SRC, dtype=BF16),
            held(SRC, 2 * H, dtype=BF16),
            held(NC, SPH, dtype=BF16),
            held(SPH, NC, dtype=BF16),
            held(NC, NC, dtype=BF16),
            held(NC, NC, dtype=BF16),
            held(SRC, NC, dtype=BF16),
            held(SRC, NC, dtype=BF16),
            held(9, 1, LANES),
            held(ITERS, 8 * EDGE, H),
            held(ITERS, n_gy, rows, LANES),
            held(ITERS, n_gy, rows, LANES),
            held(ITERS, rows, LANES),
            held(ITERS, n_gx, rows, LANES),
            held(ITERS, n_gy, rows, LANES),
            held(Q, NC),
            held(1, NC),
            held(Q, NC),
            held(Q, NC),
            held(ITERS - 1, SPH, H),
            held(1, 1, LANES),
            held(n_gx * n_gy, 1, LANES),
            dma((12,)),
            dma((ITERS, 8)),
            dma((ITERS, 8)),
            dma((8,)),
            dma((8,)),
            dma((ITERS,)),
            dma((ITERS,)),
            dma((ITERS,)),
            dma((ITERS,)),
            dma((ITERS,)),
            dma((ITERS,)),
            dma((1,)),
            dma((1,)),
        ],
        compiler_params=pltpu.CompilerParams(
            collective_id=0, has_side_effects=True, vmem_limit_bytes=60 * 1024 * 1024
        ),
        name="screening",
    )(
        start_charges,
        solute_field,
        exposure,
        owner_offset.T,
        owner_row.T,
        live_slots.T,
        coupling.T,
        cell_index.reshape(1, SPH),
        evaluation,
        projection,
        far_kernel,
    )


def solution(mesh):
    placed = (
        P(("gx", "gy"), None),
        P(("gx", "gy"), None),
        P(("gx", "gy"), None),
        P(("gx", "gy"), None),
        P(("gx", "gy"), None),
        P(("gx", "gy"), None),
        P(("gx", "gy"), None),
        P(("gx", "gy")),
        P(),
        P(),
        P(),
    )
    return jax.shard_map(
        functools.partial(per_device, mesh.shape["gx"], mesh.shape["gy"]),
        mesh=mesh,
        in_specs=placed,
        out_specs=P(("gx", "gy"), None),
        check_vma=False,
    )
```

time: 111 us -> 70.4 us (0.63)
  Pallas kernels: 99.5 us -> 68.7 us
  local copies, waits for them, and re-layouts: 11.4 us -> 1.57 us
    pallas_call x1, Pallas kernels: 99.5 us -> 68.7 us  [per_device(): pl.pallas_call(functools.partial(kernel, n_gx, n_gy), out_shape=jax.Shape...]
    unnamed x19 -> x1, local copies, waits for them, and re-layouts: 11.4 us -> 1.57 us
where the time goes in v2:
time: 70.4 us; the launch traced here: 70.3 us
  Pallas kernels  68.7 us (98%)
  local copies, waits for them, and re-layouts  1.57 us (2%)
    pallas_call x1, Pallas kernels, per_device(): pl.pallas_call(functools.partial(kernel, n_gx, n_gy), out_shape=jax.Shape...  68.7 us
    unnamed x1, local copies, waits for them, and re-layouts  1.57 us

profile of v2, /device:TPU:1, one launch (start us, length us, event | category | flops | bytes accessed | tf_op | source)
XLA Modules:
  0.0 70.3 jit_solution(10447190487441997281)
XLA Ops:
  0.0 68.7 %screening.1 = f32[256,128]{1,0:T(8,128)} custom-call(f32[256,128]{1,0:T(8,128)} %x_hbm.1, f32[256,128]{1,0:T(8,128)} %solute_hbm.1, f32[256,128]{1,0:T(8,128)} %exposure_hbm.1, s32[32,256]{1,0:T(8,128)} %bitcast.5, s32[32,256]{1,0:T(8,128)} %bitcast.6, s32[4,256]{1,0:T(4,128)} %bitcast.8, f32[32,256]{1,0:T(8,128)} %bitcast.7, s32[1,256]{1,0:T(1,128)} %bitcast.9, ...), custom_call_target="tpu_custom_call" | custom-call | tf_op jit(solution)/shard_map/screening/pallas_call | solution.py:620
  68.7 1.6 %copy.13 = f32[256,128]{1,0:T(8,128)} copy(f32[256,128]{1,0:T(8,128)} %screening.1) | data formatting | bytes 262144

commit v3 on v2

--- a/solution.py
+++ b/solution.py
@@ -26,6 +26,7 @@
 LANES = 128
 TILES = NC // LANES
 AROUND = [(dx, dy) for dx in (-1, 0, 1) for dy in (-1, 0, 1) if (dx, dy) != (0, 0)]
+FARTHEST = (0, 2, 5, 7, 1, 6, 3, 4)
 NN = (((1,), (0,)), ((), ()))
 NT = (((1,), (1,)), ((), ()))
 
@@ -167,6 +168,8 @@
     scaled,
     expanded,
     unit,
+    pair_out,
+    pair_in,
     gram_out,
     gram_in,
     load_sem,
@@ -294,9 +297,30 @@
             dst_ref=gram_in.at[step],
             send_sem=gram_send.at[0],
             recv_sem=gram_recv.at[0],
-            device_id=(lax.rem(gx + step // n_gy, n_gx), lax.rem(gy + step % n_gy, n_gy)),
+            device_id=(
+                lax.rem(gx + step // (n_gy // 2), n_gx),
+                lax.rem(gy + 2 * (step % (n_gy // 2)), n_gy),
+            ),
             device_id_type=MESH,
         )
+
+    def pair_copy():
+        return pltpu.make_async_remote_copy(
+            src_ref=pair_out.at[0],
+            dst_ref=pair_in.at[0],
+            send_sem=gram_send.at[1],
+            recv_sem=gram_recv.at[1],
+            device_id=(gx, gy + 1 - 2 * lax.rem(gy, 2)),
+            device_id_type=MESH,
+        )
+
+    def sent(k):
+        for i in range(8):
+            halo_copy(k, i).wait_send()
+        peers = pl.ds(0, n_gy - 1)
+        bytes_of(mine.at[k, peers], part_send.at[k]).wait()
+        bytes_of(mid_in.at[k, pl.ds(1, n_gx - 1)], mid_send.at[k]).wait()
+        bytes_of(whole.at[k, peers], whole_send.at[k]).wait()
 
     def prepare(k):
         first = z[k].T[:Q]
@@ -321,7 +345,7 @@
                     mine[k, t * per + j, piece : piece + 1, :] = number[:, columns]
 
     def send_halo(k):
-        for index in range(8):
+        for index in FARTHEST:
             halo_copy(k, index).start()
 
     def send_part(k):
@@ -440,15 +464,15 @@
             whigh[rows, :] = high
             wlow[rows, :] = low
 
-    each(0, SPH // block_rows, weigh)
 
     loads[5].wait()
     prepare(0)
     pl.semaphore_wait(barrier, (n_gy - 1) + (n_gx - 1) + len(corners))
+    send_part(0)
     send_halo(0)
     for i in range(8):
         cell_copy(i).start()
-    send_part(0)
+    each(0, SPH // block_rows, weigh)
 
     loads[7].wait()
     for t in range(TILES):
@@ -456,7 +480,6 @@
         high, low = split(far[rows, :])
         farhigh[rows, :] = high
         farlow[rows, :] = low
-    far_rows(0, own_cells[:, :LANES], own_cells[:, LANES:])
     expanded[...] = jnp.zeros_like(expanded)
     for load in loads[8:] + loads[6:7]:
         load.wait()
@@ -488,11 +511,20 @@
         def _():
             spread(k - 1)
 
+        @pl.when(k > 1)
+        def _():
+            expand()
+
         @pl.when(k == 1)
         def _():
             far_rows(2 * SPH, neighbour_cells(2), neighbour_cells(3))
 
         pass_on(k)
+
+        @pl.when(k == 1)
+        def _():
+            cells = cell[...].astype(F32)
+            far_rows(0, cells[:, :LANES], cells[:, LANES:])
 
         for i in range(8):
             halo_copy(k, i).wait_recv()
@@ -511,29 +543,39 @@
             put(slice(SPH, SRC), halo[k] - taken[SPH:])
 
         potential = jnp.zeros((SPH, H), F32)
-        for d in range(ND):
-            rows = slice(d * SPH, (d + 1) * SPH)
-            both = dot(whigh[rows, :], source[...])
-            sums = both[:, :H] + both[:, H:] + dot(wlow[rows, :], source[:, :H])
-            potential = potential + product(sums, evaluation_parts[d * H : (d + 1) * H])
+        for pair in range(ND // 2):
+            sums = []
+            for d in (2 * pair, 2 * pair + 1):
+                rows = slice(d * SPH, (d + 1) * SPH)
+                both = dot(whigh[rows, :], source[...])
+                low = dot(wlow[rows, :], source[:, :H])
+                sums.append(both[:, :H] + both[:, H:] + low)
+            rows = slice(2 * pair * H, 2 * (pair + 1) * H)
+            potential = potential + product(
+                jnp.concatenate(sums, axis=1), evaluation_parts[rows]
+            )
         nearby = product(potential * exposure[...], projection_parts)
         z[k + 1] = scale * (solute[...] - nearby)
 
         @pl.when(k < ITERS - 1)
         def _():
-            send_halo(k + 1)
+            @pl.when(k == 1)
+            def _():
+                send_halo(k + 1)
+
             prepare(k + 1)
             send_part(k + 1)
 
-        @pl.when(k > 0)
-        def _():
-            expand()
+            @pl.when(k != 1)
+            def _():
+                send_halo(k + 1)
 
         return carry
 
     lax.fori_loop(0, ITERS, iterate, 0)
 
     spread(ITERS - 1)
+    expand()
     pairs = [(a, b) for a in range(ITERS) for b in range(a + 1)]
     early = [y[k + 1] - y[k] for k in range(ITERS - 1)]
     height = jnp.abs(early[0])
@@ -561,15 +603,27 @@
             sums = total(change * change) if b == a else total(change * unit[b]) * ratio
             line = line + jnp.where(lane == i, sums, 0.0)
     line = jnp.where(lane == len(pairs), most, line)
+    def merged(lines):
+        tops = lines[:, len(pairs) : len(pairs) + 1]
+        most = jnp.max(tops, axis=0, keepdims=True)
+        ratio = tops / most
+        sums = jnp.sum(lines * (ratio * ratio), axis=0, keepdims=True)
+        return jnp.where(lane == len(pairs), most, sums)
+
+    pair_out[0] = line
+    pair_copy().start()
+    pair_copy().wait_recv()
+    line = merged(jnp.concatenate([line, pair_in[0]], axis=0))
     gram_out[0] = line
     gram_in[0] = line
-    everyone = n_gx * n_gy
-    each(1, everyone, lambda step: gram_copy(step).start())
-    bytes_of(gram_in.at[pl.ds(1, everyone - 1)], gram_recv.at[0]).wait()
-    lines = gram_in[...].reshape(everyone, LANES)
-    tops = lines[:, len(pairs) : len(pairs) + 1]
-    ratio = tops / jnp.max(tops, axis=0, keepdims=True)
-    line = jnp.sum(lines * (ratio * ratio), axis=0, keepdims=True)
+    chips = n_gx * n_gy // 2
+    each(1, chips, lambda step: gram_copy(step).start())
+    each(0, ITERS, sent)
+    for i in range(8):
+        cell_copy(i).wait_send()
+    pair_copy().wait_send()
+    bytes_of(gram_in.at[pl.ds(1, chips - 1)], gram_recv.at[0]).wait()
+    line = merged(gram_in[...].reshape(chips, LANES))
 
     gram = [[None] * ITERS for a in range(ITERS)]
     for i, (a, b) in enumerate(pairs):
@@ -580,18 +634,7 @@
         mixed = mixed + rho[k] * y[k]
     out_ref[...] = mixed
 
-    def sent(k):
-        for i in range(8):
-            halo_copy(k, i).wait_send()
-        peers = pl.ds(0, n_gy - 1)
-        bytes_of(mine.at[k, peers], part_send.at[k]).wait()
-        bytes_of(mid_in.at[k, pl.ds(1, n_gx - 1)], mid_send.at[k]).wait()
-        bytes_of(whole.at[k, peers], whole_send.at[k]).wait()
-
-    each(0, ITERS, sent)
-    for i in range(8):
-        cell_copy(i).wait_send()
-    bytes_of(gram_in.at[pl.ds(1, everyone - 1)], gram_send.at[0]).wait()
+    bytes_of(gram_in.at[pl.ds(1, chips - 1)], gram_send.at[0]).wait()
 
 
 def per_device(
@@ -658,7 +701,9 @@
             held(Q, NC),
             held(ITERS - 1, SPH, H),
             held(1, 1, LANES),
-            held(n_gx * n_gy, 1, LANES),
+            held(1, 1, LANES),
+            held(1, 1, LANES),
+            held(n_gx * n_gy // 2, 1, LANES),
             dma((12,)),
             dma((ITERS, 8)),
             dma((ITERS, 8)),
@@ -670,8 +715,8 @@
             dma((ITERS,)),
             dma((ITERS,)),
             dma((ITERS,)),
-            dma((1,)),
-            dma((1,)),
+            dma((2,)),
+            dma((2,)),
         ],
         compiler_params=pltpu.CompilerParams(
             collective_id=0, has_side_effects=True, vmem_limit_bytes=60 * 1024 * 1024

time: 70.4 us -> 65.6 us (0.932)
  Pallas kernels: 68.7 us -> 63.9 us
    pallas_call x1, Pallas kernels: 68.7 us -> 63.9 us  [per_device(): pl.pallas_call(functools.partial(kernel, n_gx, n_gy), out_shape=jax.Shape...]
where the time goes in v3:
time: 65.6 us; the launch traced here: 65.5 us
  Pallas kernels  63.9 us (97%)
  local copies, waits for them, and re-layouts  1.57 us (2%)
    pallas_call x1, Pallas kernels, per_device(): pl.pallas_call(functools.partial(kernel, n_gx, n_gy), out_shape=jax.Shape...  63.9 us
    unnamed x1, local copies, waits for them, and re-layouts  1.57 us

profile of v3, /device:TPU:1, one launch (start us, length us, event | category | flops | bytes accessed | tf_op | source)
XLA Modules:
  0.0 65.5 jit_solution(16227499256325158299)
XLA Ops:
  0.0 63.9 %screening.1 = f32[256,128]{1,0:T(8,128)} custom-call(f32[256,128]{1,0:T(8,128)} %x_hbm.1, f32[256,128]{1,0:T(8,128)} %solute_hbm.1, f32[256,128]{1,0:T(8,128)} %exposure_hbm.1, s32[32,256]{1,0:T(8,128)} %bitcast.5, s32[32,256]{1,0:T(8,128)} %bitcast.6, s32[4,256]{1,0:T(4,128)} %bitcast.8, f32[32,256]{1,0:T(8,128)} %bitcast.7, s32[1,256]{1,0:T(1,128)} %bitcast.9, ...), custom_call_target="tpu_custom_call" | custom-call | tf_op jit(solution)/shard_map/screening/pallas_call | solution.py:663
  63.9 1.6 %copy.13 = f32[256,128]{1,0:T(8,128)} copy(f32[256,128]{1,0:T(8,128)} %screening.1) | data formatting | bytes 262144

commit v4 on v3

--- a/solution.py
+++ b/solution.py
@@ -210,6 +210,17 @@
 
         lax.fori_loop(first, last, one, 0)
 
+    def every(count, act):
+        start = max(0, 3 * count // 8 - 1)
+        each(0, count - 1, lambda i: act(lax.rem(i + start, count - 1) + 1))
+
+    barrier = pltpu.get_barrier_semaphore()
+    every(n_gx, lambda step: greet(peer_x(step)))
+    every(n_gy, lambda step: greet(peer_y(step)))
+    corners = [i for i, (dx, dy) in enumerate(AROUND) if dx != 0 and dy != 0]
+    for i in corners:
+        greet(beside(i))
+
     loads = [
         pltpu.make_async_copy(there, here, load_sem.at[i])
         for i, (there, here) in enumerate(
@@ -231,13 +242,6 @@
     ]
     for load in loads:
         load.start()
-    barrier = pltpu.get_barrier_semaphore()
-    each(1, n_gy, lambda step: greet(peer_y(step)))
-    each(1, n_gx, lambda step: greet(peer_x(step)))
-    corners = [i for i, (dx, dy) in enumerate(AROUND) if dx != 0 and dy != 0]
-    for i in corners:
-        greet(beside(i))
-
     def bytes_of(ref, sem):
         return pltpu.make_async_copy(ref, ref, sem)
 
@@ -349,17 +353,17 @@
             halo_copy(k, index).start()
 
     def send_part(k):
-        each(1, n_gy, functools.partial(lambda k, step: part_copy(k, step).start(), k))
+        every(n_gy, lambda step: part_copy(k, step).start())
 
     def pass_on(k):
         bytes_of(part_in.at[k, pl.ds(1, n_gy - 1)], part_recv.at[k]).wait()
         plane[k] = jnp.sum(part_in[k, 1:], axis=0) + mine[k, gy]
-        each(1, n_gx, lambda step: mid_copy(k, step).start())
+        every(n_gx, lambda step: mid_copy(k, step).start())
 
     def spread(k):
         bytes_of(mid_in.at[k, pl.ds(1, n_gx - 1)], mid_recv.at[k]).wait()
         whole[k, gy] = jnp.sum(mid_in[k, 1:], axis=0) + plane[k]
-        each(1, n_gy, lambda step: whole_copy(k, step).start())
+        every(n_gy, lambda step: whole_copy(k, step).start())
 
     index = lax.broadcasted_iota(jnp.int32, (1, H), 1)
     degree = jnp.zeros((1, H), F32)
@@ -388,46 +392,43 @@
                 counts[:, columns] = whole[k, t * per, piece : piece + 1, :]
         value = moment_scale * (moments[...] - counts[...] * expanded[...])
         scaled[...] = value
-        high, low = split(value)
-        blank = jnp.zeros((H - Q, NC), BF16)
-        return jnp.concatenate([high, blank, low, blank], axis=0)
-
-    def distant(both, rows):
-        result = dot(kghigh[rows, :], both, NT)
-        return result[:, :H] + result[:, H:] + dot(kglow[rows, :], both[:H], NT)
+        return jnp.concatenate(split(value), axis=0)
+
+    def distant(both, count):
+        sums = dot(both, kghigh[:, :count])
+        sums = sums[:Q] + sums[Q:] + dot(both[:Q], kglow[:, :count])
+        blank = jnp.zeros((LANES - Q, LANES), F32)
+        blocks = [
+            jnp.concatenate([sums[:, at : at + LANES], blank], axis=0).T
+            for at in range(0, count, LANES)
+        ]
+        return jnp.concatenate(blocks, axis=0)
 
     def expand():
         high, low = split(scaled[...])
         both = dot(jnp.concatenate([high, low], axis=0), farhigh[...])
         expanded[...] = both[:Q] + both[Q:] + dot(high, farlow[...])
 
-    def far_rows(at, first_cells, second_cells):
-        cells = jnp.concatenate(
-            [
-                jnp.broadcast_to(first_cells, (LANES, LANES)).T,
-                jnp.broadcast_to(second_cells, (LANES, LANES)).T,
-            ],
-            axis=0,
-        )
-        for t in range(TILES):
-            numbers = lax.broadcasted_iota(jnp.int32, (SPH, LANES), 1) + t * LANES
-            columns = slice(t * LANES, (t + 1) * LANES)
-            onehot[:, columns] = (cells == numbers.astype(F32)).astype(F32).astype(BF16)
-        rows = slice(at, at + SPH)
+    def far_columns(at, chosen):
+        columns = slice(at, at + SPH)
 
         def one(step):
             block = pl.ds(pl.multiple_of(step * SPH, SPH), SPH)
-            kghigh[rows, block] = dot(onehot[...], farhigh[block, :], NT).astype(BF16)
-            kglow[rows, block] = dot(onehot[...], farlow[block, :], NT).astype(BF16)
+            kghigh[block, columns] = dot(farhigh[block, :], chosen[...]).astype(BF16)
+            kglow[block, columns] = dot(farlow[block, :], chosen[...]).astype(BF16)
 
         each(0, NC // SPH, one)
 
+    def belong(chosen, cells):
+        cells = jnp.broadcast_to(cells, (LANES, SPH))
+        for t in range(TILES):
+            numbers = lax.broadcasted_iota(jnp.int32, (LANES, SPH), 0) + t * LANES
+            rows = slice(t * LANES, (t + 1) * LANES)
+            chosen[rows, :] = (cells == numbers.astype(F32)).astype(F32).astype(BF16)
+
     loads[0].wait()
-    cell_row = jnp.broadcast_to(cell[...], (LANES, SPH))
-    for t in range(TILES):
-        cells = lax.broadcasted_iota(jnp.int32, (LANES, SPH), 0) + t * LANES
-        member[t * LANES : (t + 1) * LANES, :] = (cell_row == cells).astype(F32).astype(BF16)
     own_cells = cell[...].astype(F32)
+    belong(member, own_cells)
     near_cells[8] = jnp.concatenate([own_cells[:, :EDGE], own_cells[:, :EDGE]], axis=1)
 
     for i in range(1, 5):
@@ -492,8 +493,12 @@
         both = dot(high, right)
         return both[:, :H] + both[:, H:] + dot(low, right[:, :H])
 
-    def neighbour_cells(pair):
-        return jnp.where(lane < EDGE, near_cells[2 * pair], near_cells[2 * pair + 1])
+    def neighbour_cells(first):
+        pairs = [
+            jnp.where(lane < EDGE, near_cells[at], near_cells[at + 1])
+            for at in (first, first + 2)
+        ]
+        return jnp.concatenate(pairs, axis=1)
 
     def put(rows, value):
         high, low = split(value)
@@ -505,7 +510,8 @@
         def _():
             for i in range(8):
                 cell_copy(i).wait_recv()
-            far_rows(SPH, neighbour_cells(0), neighbour_cells(1))
+            belong(onehot, neighbour_cells(0))
+            far_columns(SPH, onehot)
 
         @pl.when(k > 0)
         def _():
@@ -517,14 +523,14 @@
 
         @pl.when(k == 1)
         def _():
-            far_rows(2 * SPH, neighbour_cells(2), neighbour_cells(3))
+            belong(onehot, neighbour_cells(4))
+            far_columns(2 * SPH, onehot)
 
         pass_on(k)
 
         @pl.when(k == 1)
         def _():
-            cells = cell[...].astype(F32)
-            far_rows(0, cells[:, :LANES], cells[:, LANES:])
+            far_columns(0, member)
 
         for i in range(8):
             halo_copy(k, i).wait_recv()
@@ -536,7 +542,7 @@
 
         @pl.when(k > 0)
         def _():
-            taken = distant(gathered(k - 1), slice(0, SRC))
+            taken = distant(gathered(k - 1), SRC)
             own = z[k] - taken[:SPH]
             y[k] = own
             put(slice(0, SPH), own)
@@ -591,7 +597,7 @@
         if a < ITERS - 1:
             line = line + jnp.where(lane == i, total(unit[a] * unit[b]), 0.0)
 
-    last = z[ITERS] - distant(gathered(ITERS - 1), slice(0, SPH))
+    last = z[ITERS] - distant(gathered(ITERS - 1), SPH)
     y[ITERS] = last
     change = last - y[ITERS - 1]
     most = jnp.maximum(top, largest(jnp.abs(change)))
@@ -617,7 +623,10 @@
     gram_out[0] = line
     gram_in[0] = line
     chips = n_gx * n_gy // 2
-    each(1, chips, lambda step: gram_copy(step).start())
+    columns = n_gy // 2
+    for row in sorted(range(n_gx), key=lambda row: -min(row, n_gx - row)):
+        first = row * columns
+        each(max(first, 1), first + columns, lambda step: gram_copy(step).start())
     each(0, ITERS, sent)
     for i in range(8):
         cell_copy(i).wait_send()
@@ -683,11 +692,11 @@
             held(ND * SPH, SRC, dtype=BF16),
             held(SRC, 2 * H, dtype=BF16),
             held(NC, SPH, dtype=BF16),
-            held(SPH, NC, dtype=BF16),
+            held(NC, SPH, dtype=BF16),
             held(NC, NC, dtype=BF16),
             held(NC, NC, dtype=BF16),
-            held(SRC, NC, dtype=BF16),
-            held(SRC, NC, dtype=BF16),
+            held(NC, SRC, dtype=BF16),
+            held(NC, SRC, dtype=BF16),
             held(9, 1, LANES),
             held(ITERS, 8 * EDGE, H),
             held(ITERS, n_gy, rows, LANES),
@@ -719,10 +728,13 @@
             dma((2,)),
         ],
         compiler_params=pltpu.CompilerParams(
-            collective_id=0, has_side_effects=True, vmem_limit_bytes=60 * 1024 * 1024
+            collective_id=0, has_side_effects=True, vmem_limit_bytes=48 * 1024 * 1024
         ),
         name="screening",
     )(
+        *[
+            pltpu.with_memory_space_constraint(a, pltpu.HBM)
+            for a in (
         start_charges,
         solute_field,
         exposure,
@@ -734,6 +746,8 @@
         evaluation,
         projection,
         far_kernel,
+            )
+        ]
     )
 
 

time: 65.6 us -> 62.7 us (0.956)
  Pallas kernels: 63.9 us -> 61.9 us
  local copies, waits for them, and re-layouts: 1.57 us -> 0.66 us
    pallas_call x1, Pallas kernels: 63.9 us -> 61.9 us  [per_device(): pl.pallas_call(functools.partial(kernel, n_gx, n_gy), out_shape=jax.Shape...]
    unnamed x1, local copies, waits for them, and re-layouts: 1.57 us -> 0.66 us
where the time goes in v4:
time: 62.7 us; the launch traced here: 62.6 us
  Pallas kernels  61.9 us (99%)
  local copies, waits for them, and re-layouts  0.66 us (1%)
    pallas_call x1, Pallas kernels, per_device(): pl.pallas_call(functools.partial(kernel, n_gx, n_gy), out_shape=jax.Shape...  61.9 us

profile of v4, /device:TPU:1, one launch (start us, length us, event | category | flops | bytes accessed | tf_op | source)
XLA Modules:
  0.0 62.6 jit_solution(462377465542647065)
XLA Ops:
  0.0 61.9 %screening.1 = f32[256,128]{1,0:T(8,128)S(1)} custom-call(f32[256,128]{1,0:T(8,128)} %x_hbm.1, f32[256,128]{1,0:T(8,128)} %solute_hbm.1, f32[256,128]{1,0:T(8,128)} %exposure_hbm.1, s32[32,256]{1,0:T(8,128)} %bitcast.5, s32[32,256]{1,0:T(8,128)} %bitcast.6, s32[4,256]{1,0:T(4,128)} %bitcast.8, f32[32,256]{1,0:T(8,128)} %bitcast.7, s32[1,256]{1,0:T(1,128)} %bitcast.9, ...), custom_call_target="tpu_custom_call" | custom-call | tf_op jit(solution)/shard_map/screening/pallas_call | solution.py:672
  61.9 0.7 %copy.13 = f32[256,128]{1,0:T(8,128)} copy(f32[256,128]{1,0:T(8,128)S(1)} %screening.1) | data formatting | bytes 262144

commit v5 on v4

--- a/solution.py
+++ b/solution.py
@@ -449,7 +449,7 @@
 
     block_rows = 16
 
-    def weigh(step):
+    def weigh(first, count, step):
         base = pl.multiple_of(step * block_rows, block_rows)
         held = slots[pl.ds(base, block_rows), :]
         lanes = lax.broadcasted_iota(jnp.int32, (block_rows, LANES), 1).astype(F32)
@@ -461,7 +461,8 @@
                 for t in range(SRC // LANES):
                     sums[t] = sums[t] + jnp.where(where == lanes + t * LANES, value, 0.0)
             high, low = split(jnp.concatenate(sums, axis=1))
-            rows = pl.ds(pl.multiple_of(d * SPH + base, block_rows), block_rows)
+            at = ND * first + d * count + base - first
+            rows = pl.ds(pl.multiple_of(at, block_rows), block_rows)
             whigh[rows, :] = high
             wlow[rows, :] = low
 
@@ -473,7 +474,8 @@
     send_halo(0)
     for i in range(8):
         cell_copy(i).start()
-    each(0, SPH // block_rows, weigh)
+    each(0, EDGE // block_rows, functools.partial(weigh, 0, EDGE))
+    each(EDGE // block_rows, SPH // block_rows, functools.partial(weigh, EDGE, SPH - EDGE))
 
     loads[7].wait()
     for t in range(TILES):
@@ -505,6 +507,21 @@
         source[rows, :H] = high
         source[rows, H:] = low
 
+    def update(k, *ranges):
+        begin, end = ranges[0][0], sum(ranges[-1])
+        rows = slice(ND * begin, ND * end)
+        both = dot(whigh[rows, :], source[...])
+        sums = both[:, :H] + both[:, H:] + dot(wlow[rows, :], source[:, :H])
+        blocks = []
+        for first, count in ranges:
+            at = ND * (first - begin)
+            parts = [sums[at + d * count : at + (d + 1) * count] for d in range(ND)]
+            blocks.append(jnp.concatenate(parts, axis=1))
+        chosen = slice(begin, end)
+        potential = product(jnp.concatenate(blocks, axis=0), evaluation_parts)
+        nearby = product(potential * exposure[chosen, :], projection_parts)
+        z[k + 1, chosen, :] = scale * (solute[chosen, :] - nearby)
+
     def iterate(k, carry):
         @pl.when(k == 1)
         def _():
@@ -548,27 +565,20 @@
             put(slice(0, SPH), own)
             put(slice(SPH, SRC), halo[k] - taken[SPH:])
 
-        potential = jnp.zeros((SPH, H), F32)
-        for pair in range(ND // 2):
-            sums = []
-            for d in (2 * pair, 2 * pair + 1):
-                rows = slice(d * SPH, (d + 1) * SPH)
-                both = dot(whigh[rows, :], source[...])
-                low = dot(wlow[rows, :], source[:, :H])
-                sums.append(both[:, :H] + both[:, H:] + low)
-            rows = slice(2 * pair * H, 2 * (pair + 1) * H)
-            potential = potential + product(
-                jnp.concatenate(sums, axis=1), evaluation_parts[rows]
-            )
-        nearby = product(potential * exposure[...], projection_parts)
-        z[k + 1] = scale * (solute[...] - nearby)
+        edge, others = (0, EDGE), (EDGE, SPH - EDGE)
+
+        @pl.when(k == 1)
+        def _():
+            update(k, edge)
+            send_halo(k + 1)
+            update(k, others)
+
+        @pl.when(k != 1)
+        def _():
+            update(k, edge, others)
 
         @pl.when(k < ITERS - 1)
         def _():
-            @pl.when(k == 1)
-            def _():
-                send_halo(k + 1)
-
             prepare(k + 1)
             send_part(k + 1)
 

time: 62.7 us -> 62.3 us (level)
  no operation moved by 1% of the time
where the time goes in v5:
time: 62.3 us; the launch traced here: 62.2 us
  Pallas kernels  61.6 us (99%)
  local copies, waits for them, and re-layouts  0.66 us (1%)
    pallas_call x1, Pallas kernels, per_device(): pl.pallas_call(functools.partial(kernel, n_gx, n_gy), out_shape=jax.Shape...  61.6 us

profile of v5, /device:TPU:1, one launch (start us, length us, event | category | flops | bytes accessed | tf_op | source)
XLA Modules:
  0.0 62.2 jit_solution(10337633242804867004)
XLA Ops:
  0.0 61.6 %screening.1 = f32[256,128]{1,0:T(8,128)S(1)} custom-call(f32[256,128]{1,0:T(8,128)} %x_hbm.1, f32[256,128]{1,0:T(8,128)} %solute_hbm.1, f32[256,128]{1,0:T(8,128)} %exposure_hbm.1, s32[32,256]{1,0:T(8,128)} %bitcast.5, s32[32,256]{1,0:T(8,128)} %bitcast.6, s32[4,256]{1,0:T(4,128)} %bitcast.8, f32[32,256]{1,0:T(8,128)} %bitcast.7, s32[1,256]{1,0:T(1,128)} %bitcast.9, ...), custom_call_target="tpu_custom_call" | custom-call | tf_op jit(solution)/shard_map/screening/pallas_call | solution.py:682
  61.6 0.7 %copy.13 = f32[256,128]{1,0:T(8,128)} copy(f32[256,128]{1,0:T(8,128)S(1)} %screening.1) | data formatting | bytes 262144
